TPU v7x, 512 devices: a whole 4x8x8 slice. The times are simulated.
512 devices in a mesh: shell: 64 (over x, y, z_lo), lat: 8 (over z_hi, core).
Axes of the slice: x: 4, y: 8, z: 8 (z_hi: 4, z_lo: 2; z = z_hi * 2 + z_lo), core: 2. Of those that a mesh axis runs over, the one named last changes fastest.
Arguments:
- advective_warming: bfloat16 [256, 768, 1536], P('shell', 'lat'), may hold values from -6 to 6
- associated_polynomial_table: bfloat16 [128, 768, 512], P(None, 'lat', 'shell'), may hold values from -12 to 12, as said below
- thermal_field: float32 [512, 128, 2, 256], P('shell', 'lat'), may hold values from -6 to 6
- operator_reciprocal: float32 [512, 256, 256], P('shell'), may hold values from -1 to 3, as said below
Outputs:
- new_temperature: float32 [512, 128, 2, 256], P('shell', 'lat')
Inputs may be any that keep to these rules, and one draw needn't show every extreme that they name: `associated_polynomial_table`: zero wherever the degree l is below the order j * 4. `operator_reciprocal`: one matrix of order 256 for each degree.
All inputs are finite; a program needn't handle non-finite values.
Results may differ from a plain program's by a relative error of at most 0.007.
Values may be sent and summed in bfloat16 or wider, within the bound.
A program may use at most 128 MiB of HBM per device.

v0:
```python
import math
import jax
import jax.numpy as jnp
import numpy as np
from jax import lax
from jax.sharding import Mesh, PartitionSpec as P

backward_euler_update = 0.5


def analysis_rows(orders, stride, longitudes):
    phase = np.arange(orders)[:, None] * stride * np.arange(longitudes)[None, :] % longitudes
    angles = phase.astype(np.float32) * np.float32(2.0 * math.pi / longitudes)
    stacked = np.stack([np.cos(angles), -np.sin(angles)], axis=1) / np.float32(longitudes)
    return jnp.asarray(stacked.reshape(2 * orders, longitudes)).astype(jnp.bfloat16)


def shards(advective_warming, table, thermal_field, operator_reciprocal):
    radial_levels, bands, longitudes = advective_warming.shape
    orders = table.shape[0]
    own_degrees = table.shape[2]
    degrees = own_degrees * lax.axis_size("x") * lax.axis_size("g")
    table = lax.all_to_all(table, "lat", split_axis=0, concat_axis=1, tiled=True)
    table = lax.all_to_all(table, "g", split_axis=0, concat_axis=2, tiled=True)
    table = lax.all_gather(table, "x", axis=2, tiled=True)
    analysis = analysis_rows(orders, degrees // orders, longitudes)
    fourier = lax.dot_general(
        analysis,
        advective_warming.reshape(radial_levels * bands, longitudes),
        (((1,), (1,)), ((), ())),
        preferred_element_type=jnp.float32,
    )
    fourier = fourier.astype(jnp.bfloat16).reshape(orders, 2, radial_levels, bands)
    fourier = lax.all_to_all(fourier, "lat", split_axis=0, concat_axis=3, tiled=True)
    fourier = lax.all_to_all(fourier, "g", split_axis=0, concat_axis=2, tiled=True)
    block = jnp.einsum("mcrt,mtl->mcrl", fourier, table, preferred_element_type=jnp.float32)
    own_levels = block.shape[2]
    block = lax.all_to_all(
        block.astype(jnp.bfloat16), ("x", "g"), split_axis=3, concat_axis=0, tiled=True
    ).astype(jnp.float32)
    block = block.reshape(-1, thermal_field.shape[1], 2, own_levels, own_degrees)
    block = jnp.transpose(block, (4, 1, 2, 0, 3)).reshape(thermal_field.shape)
    forcing = thermal_field + backward_euler_update * block
    return jnp.einsum(
        "lij,lmcj->lmci", operator_reciprocal, forcing, precision=lax.Precision.HIGHEST
    )


def solution(mesh):
    shells, lats = mesh.devices.shape
    finer = Mesh(mesh.devices.reshape(4, shells // 4, lats), ("x", "g", "lat"))
    shell = ("x", "g")
    in_specs = (
        P(shell, "lat", None),
        P(None, "lat", shell),
        P(shell, "lat", None, None),
        P(shell, None, None),
    )
    out_specs = P(shell, "lat", None, None)
    return jax.shard_map(
        shards, mesh=finer, in_specs=in_specs, out_specs=out_specs, check_vma=False
    )
```

profile of v0, /device:TPU:8, one launch (start us, length us, event | category | flops | bytes accessed | tf_op | source)
XLA Modules:
  0.0 108.8 jit_solution(15241552492936182516)
XLA Ops:
  0.0 2.2 %convolution_convert_fusion = bf16[256,384]{1,0:T(8,128)(2,1)S(1)} fusion(bf16[256,1536]{1,0:T(8,128)(2,1)} %constant.9, bf16[384,1536]{1,0:T(8,128)(2,1)} %bitcast.51), kind=kOutput, calls=%fused_computation.2 | convolution fusion | flops 302088192 | bytes 2162688 | tf_op jit(solution)/shard_map/dot_general | solution.py:27
  2.3 0.9 reshape.26
  3.1 10.3 %all-to-all-start = ((bf16[128,2,4,96]{3,2,1,0:T(4,128)(2,1)}), bf16[128,2,4,96]{3,2,1,0:T(4,128)(2,1)S(1)}, u32[]{:S(2)}, u32[]{:S(2)}) async-start(bf16[128,2,4,96]{3,2,1,0:T(4,128)(2,1)} %reshape.26), calls=%async_computation | async-start | bytes 524288 | tf_op jit(solution)/shard_map/all_to_all | solution.py:34
  13.5 0.9 copy.28
  14.4 11.8 %all-to-all-done = bf16[128,2,4,96]{3,2,1,0:T(4,128)(2,1)S(1)} async-done(((bf16[128,2,4,96]{3,2,1,0:T(4,128)(2,1)}), bf16[128,2,4,96]{3,2,1,0:T(4,128)(2,1)S(1)}, u32[]{:S(2)}, u32[]{:S(2)}) %all-to-all-start) | async-done | bytes 196640 | tf_op jit(solution)/shard_map/all_to_all | solution.py:34
  26.2 3.4 %all-to-all-start.2 = ((bf16[128,96,8]{1,2,0:T(8,128)(2,1)}), bf16[128,96,8]{1,2,0:T(8,128)(2,1)S(1)}, u32[]{:S(2)}, u32[]{:S(2)}) async-start(bf16[128,96,8]{1,2,0:T(8,128)(2,1)} %copy.28), calls=%async_computation.2 | async-start | bytes 524288 | tf_op jit(solution)/shard_map/all_to_all | solution.py:23
  29.6 0.3 copy.26
  29.9 0.9 all_to_all.60
  30.9 10.8 %all-to-all-done.2 = bf16[128,96,8]{1,2,0:T(8,128)(2,1)S(1)} async-done(((bf16[128,96,8]{1,2,0:T(8,128)(2,1)}), bf16[128,96,8]{1,2,0:T(8,128)(2,1)S(1)}, u32[]{:S(2)}, u32[]{:S(2)}) %all-to-all-start.2) | async-done | bytes 196640 | tf_op jit(solution)/shard_map/all_to_all | solution.py:23
  41.6 8.3 %all-to-all-start.1 = ((bf16[16,2,4,768]{3,2,1,0:T(4,128)(2,1)}), bf16[16,2,4,768]{3,2,1,0:T(4,128)(2,1)S(1)}, u32[]{:S(2)}, u32[]{:S(2)}) async-start(bf16[16,2,4,768]{3,2,1,0:T(4,128)(2,1)} %all_to_all.60), calls=%async_computation.1 | async-start | bytes 393216 | tf_op jit(solution)/shard_map/all_to_all | solution.py:35
  49.9 0.2 copy.29
  50.1 0.9 all_to_all.67
  51.0 7.7 %all-to-all-done.1 = bf16[16,2,4,768]{3,2,1,0:T(4,128)(2,1)S(1)} async-done(((bf16[16,2,4,768]{3,2,1,0:T(4,128)(2,1)}), bf16[16,2,4,768]{3,2,1,0:T(4,128)(2,1)S(1)}, u32[]{:S(2)}, u32[]{:S(2)}) %all-to-all-start.1) | async-done | bytes 196640 | tf_op jit(solution)/shard_map/all_to_all | solution.py:35
  58.8 4.8 %all-to-all-start.3 = ((bf16[16,768,8]{1,2,0:T(8,128)(2,1)}), bf16[16,768,8]{1,2,0:T(8,128)(2,1)S(1)}, u32[]{:S(2)}, u32[]{:S(2)}) async-start(bf16[16,768,8]{1,2,0:T(8,128)(2,1)} %all_to_all.67), calls=%async_computation.3 | async-start | bytes 393216 | tf_op jit(solution)/shard_map/all_to_all | solution.py:24
  63.7 8.7 %all-to-all-done.3 = bf16[16,768,8]{1,2,0:T(8,128)(2,1)S(1)} async-done(((bf16[16,768,8]{1,2,0:T(8,128)(2,1)}), bf16[16,768,8]{1,2,0:T(8,128)(2,1)S(1)}, u32[]{:S(2)}, u32[]{:S(2)}) %all-to-all-start.3) | async-done | bytes 196640 | tf_op jit(solution)/shard_map/all_to_all | solution.py:24
  72.5 16.0 %all_gather.3 = bf16[1,768,512]{2,1,0:T(8,128)(2,1)S(1)} all-gather(bf16[1,768,128]{2,1,0:T(8,128)(2,1)S(1)} %copy.30), channel_id=1, replica_groups=mesh['x'=4,'g'=16,'lat'=8] {'x'}, dimensions={2}, use_global_device_ids=true | all-gather | bytes 983040 | tf_op jit(solution)/shard_map/all_gather | solution.py:25
  88.5 0.3 fusion.2
  88.9 0.2 reshape.34
  89.1 15.6 %all_to_all.78 = bf16[64,2,512]{2,1,0:T(2,128)(2,1)S(1)} all-to-all(bf16[64,2,512]{2,1,0:T(2,128)(2,1)S(1)} %reshape.34), channel_id=1, replica_groups=mesh['x'=4,'g'=16,'lat'=8] {'x','g'}, dimensions={0} | all-to-all | bytes 262144 | tf_op jit(solution)/shard_map/all_to_all | solution.py:38
  104.7 0.2 reshape.35
  105.0 0.3 copy.33
  105.3 0.4 mul.23
  105.9 2.0 %fusion = f32[8,16,2,256]{3,1,2,0:T(8,128)S(1)} fusion(f32[8,256,256]{2,1,0:T(8,128)S(1)} %copy-done, f32[8,16,2,256]{3,2,1,0:T(2,128)S(1)} %add.3), kind=kOutput, calls=%fused_computation | convolution fusion | flops 201326592 | bytes 2621440 | tf_op jit(solution)/shard_map/lij,lmcj->lmci/dot_general | solution.py:44
  107.9 0.9 copy.35
  (12 shorter events, 0.6 us)
Async XLA Ops:
  0.0 105.9 %copy-start = (f32[8,256,256]{2,1,0:T(8,128)S(1)}, f32[8,256,256]{2,1,0:T(8,128)}, u32[]{:S(2)}) copy-start(f32[8,256,256]{2,1,0:T(8,128)} %param.8) | copy-start | bytes 6291460
  0.0 13.4 %copy-start.2 = (bf16[128,96,8]{0,2,1:T(8,128)(2,1)S(1)}, bf16[128,96,8]{0,2,1:T(8,128)(2,1)}, u32[]{:S(2)}) copy-start(bf16[128,96,8]{0,2,1:T(8,128)(2,1)} %param.6) | copy-start | bytes 589828
  3.1 23.1 %all-to-all-start = ((bf16[128,2,4,96]{3,2,1,0:T(4,128)(2,1)}), bf16[128,2,4,96]{3,2,1,0:T(4,128)(2,1)S(1)}, u32[]{:S(2)}, u32[]{:S(2)}) async-start(bf16[128,2,4,96]{3,2,1,0:T(4,128)(2,1)} %reshape.26), calls=%async_computation | async-start | bytes 524288 | tf_op jit(solution)/shard_map/all_to_all | solution.py:34
  26.2 15.4 %all-to-all-start.2 = ((bf16[128,96,8]{1,2,0:T(8,128)(2,1)}), bf16[128,96,8]{1,2,0:T(8,128)(2,1)S(1)}, u32[]{:S(2)}, u32[]{:S(2)}) async-start(bf16[128,96,8]{1,2,0:T(8,128)(2,1)} %copy.28), calls=%async_computation.2 | async-start | bytes 524288 | tf_op jit(solution)/shard_map/all_to_all | solution.py:23
  41.6 17.1 %all-to-all-start.1 = ((bf16[16,2,4,768]{3,2,1,0:T(4,128)(2,1)}), bf16[16,2,4,768]{3,2,1,0:T(4,128)(2,1)S(1)}, u32[]{:S(2)}, u32[]{:S(2)}) async-start(bf16[16,2,4,768]{3,2,1,0:T(4,128)(2,1)} %all_to_all.60), calls=%async_computation.1 | async-start | bytes 393216 | tf_op jit(solution)/shard_map/all_to_all | solution.py:35
  58.8 13.6 %all-to-all-start.3 = ((bf16[16,768,8]{1,2,0:T(8,128)(2,1)}), bf16[16,768,8]{1,2,0:T(8,128)(2,1)S(1)}, u32[]{:S(2)}, u32[]{:S(2)}) async-start(bf16[16,768,8]{1,2,0:T(8,128)(2,1)} %all_to_all.67), calls=%async_computation.3 | async-start | bytes 393216 | tf_op jit(solution)/shard_map/all_to_all | solution.py:24
  88.8 17.0 %copy-start.1 = (f32[8,16,2,256]{3,2,1,0:T(2,128)S(1)}, f32[8,16,2,256]{3,2,1,0:T(2,128)}, u32[]{:S(2)}) copy-start(f32[8,16,2,256]{3,2,1,0:T(2,128)} %param.7) | copy-start | bytes 786436
where the time goes:
time: 109 us
  waiting for transfers between devices  39 us (36%)
  blocking collectives  31.5 us (29%)
  starting transfers between devices  26.8 us (25%)
  local copies, waits for them, and re-layouts  6.65 us (6%)
  matrix products  4.53 us (4%)
    all_gather x1, blocking collectives, shards(): table = lax.all_gather(table, 'x', axis=2, tiled=True)  16 us
    all_to_all x1, blocking collectives, shards(): lax.all_to_all(block.astype(jnp.bfloat16), ('x', 'g'), split_axis=3, conc...  15.6 us
    all_to_all x1, waiting for transfers between devices, shards(): lax.all_to_all(fourier, 'lat', split_axis=0, concat_axis=3, tiled=True)  11.8 us
    all_to_all x1, waiting for transfers between devices, shards(): lax.all_to_all(table, 'lat', split_axis=0, concat_axis=1, tiled=True)  10.8 us
    all_to_all x1, starting transfers between devices, shards(): lax.all_to_all(fourier, 'lat', split_axis=0, concat_axis=3, tiled=True)  10.3 us
    all_to_all x1, waiting for transfers between devices, shards(): table = lax.all_to_all(table, 'g', split_axis=0, concat_axis=2, tiled=True)  8.67 us
    all_to_all x1, starting transfers between devices, shards(): lax.all_to_all(fourier, 'g', split_axis=0, concat_axis=2, tiled=True)  8.3 us
    all_to_all x1, waiting for transfers between devices, shards(): lax.all_to_all(fourier, 'g', split_axis=0, concat_axis=2, tiled=True)  7.73 us
  transfers between devices with their start and end apart: 4, of which 4 were waited for; matrix products, arithmetic and copies ran while one was open for 1% of the time, Pallas kernels for 0%

commit v1 on v0

--- a/solution.py
+++ b/solution.py
@@ -6,6 +6,13 @@
 from jax.sharding import Mesh, PartitionSpec as P
 
 backward_euler_update = 0.5
+
+
+def touch_steps_all(obj):
+    then = jnp.stack([obj for _ in range(jax.lax.axis_size("x"))], 0)
+    carry = jax.lax.all_to_all(then, "x", 0, 0)
+    ready = jnp.concatenate(carry, 2)
+    return ready
 
 
 def analysis_rows(orders, stride, longitudes):
@@ -22,7 +29,7 @@
     degrees = own_degrees * lax.axis_size("x") * lax.axis_size("g")
     table = lax.all_to_all(table, "lat", split_axis=0, concat_axis=1, tiled=True)
     table = lax.all_to_all(table, "g", split_axis=0, concat_axis=2, tiled=True)
-    table = lax.all_gather(table, "x", axis=2, tiled=True)
+    table = touch_steps_all(table)
     analysis = analysis_rows(orders, degrees // orders, longitudes)
     fourier = lax.dot_general(
         analysis,

time: 109 us -> 110 us (level)
  blocking collectives: 31.5 us -> 14.9 us
  waiting for transfers between devices: 39 us -> 46.3 us
  local copies, waits for them, and re-layouts: 6.65 us -> 11.9 us
  starting transfers between devices: 26.8 us -> 31.1 us
    all_gather x1 -> x0, blocking collectives: 16 us -> none  [shards(): table = lax.all_gather(table, 'x', axis=2, tiled=True)]
    all_to_all x0 -> x1, waiting for transfers between devices: none -> 9.36 us  [touch_steps_all(): carry = jax.lax.all_to_all(then, 'x', 0, 0)]
    all_to_all x1, starting transfers between devices: 3.41 us -> 10.3 us  [shards(): lax.all_to_all(table, 'lat', split_axis=0, concat_axis=1, tiled=True)]
    all_to_all x1, starting transfers between devices: 10.3 us -> 3.41 us  [shards(): lax.all_to_all(fourier, 'lat', split_axis=0, concat_axis=3, tiled=True)]
    all_to_all x0 -> x1, starting transfers between devices: none -> 4.29 us  [touch_steps_all(): carry = jax.lax.all_to_all(then, 'x', 0, 0)]
    all_to_all x1, starting transfers between devices: 4.8 us -> 8.3 us  [shards(): table = lax.all_to_all(table, 'g', split_axis=0, concat_axis=2, tiled=True)]
    all_to_all x1, starting transfers between devices: 8.3 us -> 4.8 us  [shards(): lax.all_to_all(fourier, 'g', split_axis=0, concat_axis=2, tiled=True)]
    another operation x0 -> x4, local copies, waits for them, and re-layouts: none -> 2.85 us
  transfers between devices with their start and end apart: 4 -> 5, of which waited for: 4 -> 5; matrix products, arithmetic and copies ran while one was open for 1% -> 3% of each run, Pallas kernels for 0% -> 0%
where the time goes in v1:
time: 110 us; the launch traced here: 109 us
  waiting for transfers between devices  46.3 us (42%)
  starting transfers between devices  31.1 us (28%)
  blocking collectives  14.9 us (14%)
  local copies, waits for them, and re-layouts  11.9 us (11%)
  matrix products  4.38 us (4%)
    all_to_all x1, blocking collectives, shards(): lax.all_to_all(block.astype(jnp.bfloat16), ('x', 'g'), split_axis=3, conc...  14.9 us
    all_to_all x1, waiting for transfers between devices, shards(): lax.all_to_all(fourier, 'lat', split_axis=0, concat_axis=3, tiled=True)  10.9 us
    all_to_all x1, starting transfers between devices, shards(): lax.all_to_all(table, 'lat', split_axis=0, concat_axis=1, tiled=True)  10.3 us
    all_to_all x1, waiting for transfers between devices, shards(): lax.all_to_all(table, 'lat', split_axis=0, concat_axis=1, tiled=True)  9.77 us
    all_to_all x1, waiting for transfers between devices, touch_steps_all(): carry = jax.lax.all_to_all(then, 'x', 0, 0)  9.36 us
    all_to_all x1, waiting for transfers between devices, shards(): lax.all_to_all(fourier, 'g', split_axis=0, concat_axis=2, tiled=True)  8.64 us
    all_to_all x1, starting transfers between devices, shards(): table = lax.all_to_all(table, 'g', split_axis=0, concat_axis=2, tiled=True)  8.3 us
    all_to_all x1, waiting for transfers between devices, shards(): table = lax.all_to_all(table, 'g', split_axis=0, concat_axis=2, tiled=True)  7.55 us
  transfers between devices with their start and end apart: 5, of which 5 were waited for; matrix products, arithmetic and copies ran while one was open for 3% of the time, Pallas kernels for 0%

profile of v1, /device:TPU:8, one launch (start us, length us, event | category | flops | bytes accessed | tf_op | source)
XLA Modules:
  0.0 108.9 jit_solution(15545663367335353828)
XLA Ops:
  0.0 2.0 %copy.20 = bf16[128,96,8]{1,2,0:T(8,128)(2,1)} copy(bf16[128,96,8]{0,2,1:T(8,128)(2,1)} %param.6) | data formatting | bytes 393216 | tf_op args[1]
  2.0 10.3 %all-to-all-start.2 = ((bf16[128,96,8]{1,2,0:T(8,128)(2,1)}), bf16[128,96,8]{1,2,0:T(8,128)(2,1)S(1)}, u32[]{:S(2)}, u32[]{:S(2)}) async-start(bf16[128,96,8]{1,2,0:T(8,128)(2,1)} %copy.20), calls=%async_computation.2 | async-start | bytes 524288 | tf_op jit(solution)/shard_map/all_to_all | solution.py:30
  12.3 2.1 %convolution_convert_fusion = bf16[256,384]{1,0:T(8,128)(2,1)S(1)} fusion(bf16[256,1536]{1,0:T(8,128)(2,1)} %constant.9, bf16[384,1536]{1,0:T(8,128)(2,1)} %bitcast.50), kind=kOutput, calls=%fused_computation.2 | convolution fusion | flops 302088192 | bytes 2162688 | tf_op jit(solution)/shard_map/dot_general | solution.py:34
  14.4 0.9 reshape.36
  15.3 9.8 %all-to-all-done.2 = bf16[128,96,8]{1,2,0:T(8,128)(2,1)S(1)} async-done(((bf16[128,96,8]{1,2,0:T(8,128)(2,1)}), bf16[128,96,8]{1,2,0:T(8,128)(2,1)S(1)}, u32[]{:S(2)}, u32[]{:S(2)}) %all-to-all-start.2) | async-done | bytes 196640 | tf_op jit(solution)/shard_map/all_to_all | solution.py:30
  25.1 3.4 %all-to-all-start = ((bf16[128,2,4,96]{3,2,1,0:T(4,128)(2,1)}), bf16[128,2,4,96]{3,2,1,0:T(4,128)(2,1)S(1)}, u32[]{:S(2)}, u32[]{:S(2)}) async-start(bf16[128,2,4,96]{3,2,1,0:T(4,128)(2,1)} %reshape.36), calls=%async_computation | async-start | bytes 524288 | tf_op jit(solution)/shard_map/all_to_all | solution.py:41
  28.7 0.9 all_to_all.68
  29.6 10.9 %all-to-all-done = bf16[128,2,4,96]{3,2,1,0:T(4,128)(2,1)S(1)} async-done(((bf16[128,2,4,96]{3,2,1,0:T(4,128)(2,1)}), bf16[128,2,4,96]{3,2,1,0:T(4,128)(2,1)S(1)}, u32[]{:S(2)}, u32[]{:S(2)}) %all-to-all-start) | async-done | bytes 196640 | tf_op jit(solution)/shard_map/all_to_all | solution.py:41
  40.5 8.3 %all-to-all-start.3 = ((bf16[16,768,8]{1,2,0:T(8,128)(2,1)}), bf16[16,768,8]{1,2,0:T(8,128)(2,1)S(1)}, u32[]{:S(2)}, u32[]{:S(2)}) async-start(bf16[16,768,8]{1,2,0:T(8,128)(2,1)} %all_to_all.68), calls=%async_computation.3 | async-start | bytes 393216 | tf_op jit(solution)/shard_map/all_to_all | solution.py:31
  48.8 0.3 copy.18
  49.2 0.9 all_to_all.61
  50.1 7.5 %all-to-all-done.3 = bf16[16,768,8]{1,2,0:T(8,128)(2,1)S(1)} async-done(((bf16[16,768,8]{1,2,0:T(8,128)(2,1)}), bf16[16,768,8]{1,2,0:T(8,128)(2,1)S(1)}, u32[]{:S(2)}, u32[]{:S(2)}) %all-to-all-start.3) | async-done | bytes 196640 | tf_op jit(solution)/shard_map/all_to_all | solution.py:31
  57.6 4.8 %all-to-all-start.1 = ((bf16[16,2,4,768]{3,2,1,0:T(4,128)(2,1)}), bf16[16,2,4,768]{3,2,1,0:T(4,128)(2,1)S(1)}, u32[]{:S(2)}, u32[]{:S(2)}) async-start(bf16[16,2,4,768]{3,2,1,0:T(4,128)(2,1)} %all_to_all.61), calls=%async_computation.1 | async-start | bytes 393216 | tf_op jit(solution)/shard_map/all_to_all | solution.py:42
  62.6 8.6 %all-to-all-done.1 = bf16[16,2,4,768]{3,2,1,0:T(4,128)(2,1)S(1)} async-done(((bf16[16,2,4,768]{3,2,1,0:T(4,128)(2,1)}), bf16[16,2,4,768]{3,2,1,0:T(4,128)(2,1)S(1)}, u32[]{:S(2)}, u32[]{:S(2)}) %all-to-all-start.1) | async-done | bytes 196640 | tf_op jit(solution)/shard_map/all_to_all | solution.py:42
  71.3 1.0 stack.10
  72.2 4.3 %all-to-all-start.4 = ((bf16[4,1,768,128]{3,2,1,0:T(8,128)(2,1)}), bf16[4,1,768,128]{3,2,1,0:T(8,128)(2,1)S(1)}, u32[]{:S(2)}, u32[]{:S(2)}) async-start(bf16[4,1,768,128]{3,2,1,0:T(8,128)(2,1)} %stack.10), calls=%async_computation.4 | async-start | bytes 1572864 | tf_op jit(solution)/shard_map/all_to_all | solution.py:13
  76.7 9.4 %all-to-all-done.4 = bf16[4,1,768,128]{3,2,1,0:T(8,128)(2,1)S(1)} async-done(((bf16[4,1,768,128]{3,2,1,0:T(8,128)(2,1)}), bf16[4,1,768,128]{3,2,1,0:T(8,128)(2,1)S(1)}, u32[]{:S(2)}, u32[]{:S(2)}) %all-to-all-start.4) | async-done | bytes 786464 | tf_op jit(solution)/shard_map/all_to_all | solution.py:13
  86.0 1.5 %copy.23 = bf16[1,768,4,128]{3,2,1,0:T(4,128)(2,1)} copy(bf16[1,768,4,128]{3,1,0,2:T(8,128)(2,1)S(1)} %bitcast.42) | data formatting | bytes 1572864 | tf_op jit(solution)/shard_map/reshape | solution.py:14
  87.5 1.6 %reshape.43 = bf16[768,512,1]{1,0,2:T(8,128)(2,1)S(1)} reshape(bf16[1,768,4,128]{3,2,1,0:T(4,128)(2,1)} %copy.23) | data formatting | bytes 1572864 | tf_op jit(solution)/shard_map/reshape.3
  89.8 14.9 %all_to_all.80 = bf16[64,2,512]{2,1,0:T(2,128)(2,1)S(1)} all-to-all(bf16[64,2,512]{2,1,0:T(2,128)(2,1)S(1)} %reshape.46), channel_id=1, replica_groups=mesh['x'=4,'g'=16,'lat'=8] {'x','g'}, dimensions={0} | all-to-all | bytes 262144 | tf_op jit(solution)/shard_map/all_to_all | solution.py:45
  105.0 0.3 copy.26
  105.4 0.4 mul.23
  106.0 2.0 %fusion = f32[8,16,2,256]{3,1,2,0:T(8,128)S(1)} fusion(f32[8,256,256]{2,1,0:T(8,128)S(1)} %copy-done, f32[8,16,2,256]{3,2,1,0:T(2,128)S(1)} %add.3), kind=kOutput, calls=%fused_computation | convolution fusion | flops 201326592 | bytes 2621440 | tf_op jit(solution)/shard_map/lij,lmcj->lmci/dot_general | solution.py:51
  108.0 0.9 copy.28
  (14 shorter events, 1.5 us)
Async XLA Ops:
  0.0 106.0 %copy-start = (f32[8,256,256]{2,1,0:T(8,128)S(1)}, f32[8,256,256]{2,1,0:T(8,128)}, u32[]{:S(2)}) copy-start(f32[8,256,256]{2,1,0:T(8,128)} %param.8) | copy-start | bytes 6291460
  2.0 23.1 %all-to-all-start.2 = ((bf16[128,96,8]{1,2,0:T(8,128)(2,1)}), bf16[128,96,8]{1,2,0:T(8,128)(2,1)S(1)}, u32[]{:S(2)}, u32[]{:S(2)}) async-start(bf16[128,96,8]{1,2,0:T(8,128)(2,1)} %copy.20), calls=%async_computation.2 | async-start | bytes 524288 | tf_op jit(solution)/shard_map/all_to_all | solution.py:30
  25.1 15.4 %all-to-all-start = ((bf16[128,2,4,96]{3,2,1,0:T(4,128)(2,1)}), bf16[128,2,4,96]{3,2,1,0:T(4,128)(2,1)S(1)}, u32[]{:S(2)}, u32[]{:S(2)}) async-start(bf16[128,2,4,96]{3,2,1,0:T(4,128)(2,1)} %reshape.36), calls=%async_computation | async-start | bytes 524288 | tf_op jit(solution)/shard_map/all_to_all | solution.py:41
  40.5 17.1 %all-to-all-start.3 = ((bf16[16,768,8]{1,2,0:T(8,128)(2,1)}), bf16[16,768,8]{1,2,0:T(8,128)(2,1)S(1)}, u32[]{:S(2)}, u32[]{:S(2)}) async-start(bf16[16,768,8]{1,2,0:T(8,128)(2,1)} %all_to_all.68), calls=%async_computation.3 | async-start | bytes 393216 | tf_op jit(solution)/shard_map/all_to_all | solution.py:31
  57.6 13.6 %all-to-all-start.1 = ((bf16[16,2,4,768]{3,2,1,0:T(4,128)(2,1)}), bf16[16,2,4,768]{3,2,1,0:T(4,128)(2,1)S(1)}, u32[]{:S(2)}, u32[]{:S(2)}) async-start(bf16[16,2,4,768]{3,2,1,0:T(4,128)(2,1)} %all_to_all.61), calls=%async_computation.1 | async-start | bytes 393216 | tf_op jit(solution)/shard_map/all_to_all | solution.py:42
  72.2 13.8 %all-to-all-start.4 = ((bf16[4,1,768,128]{3,2,1,0:T(8,128)(2,1)}), bf16[4,1,768,128]{3,2,1,0:T(8,128)(2,1)S(1)}, u32[]{:S(2)}, u32[]{:S(2)}) async-start(bf16[4,1,768,128]{3,2,1,0:T(8,128)(2,1)} %stack.10), calls=%async_computation.4 | async-start | bytes 1572864 | tf_op jit(solution)/shard_map/all_to_all | solution.py:13
  89.5 16.3 %copy-start.1 = (f32[8,16,2,256]{3,2,1,0:T(2,128)S(1)}, f32[8,16,2,256]{3,2,1,0:T(2,128)}, u32[]{:S(2)}) copy-start(f32[8,16,2,256]{3,2,1,0:T(2,128)} %param.7) | copy-start | bytes 786436
